TPU v7x, 128 devices: a whole 4x4x4 slice. The times are simulated.
128 devices in a mesh: dp: 16 (over z, y), cent: 8 (over x, core).
Axes of the slice: x: 4, y: 4, z: 4, core: 2. Of those that a mesh axis runs over, the one named last changes fastest.
Arguments:
- embeddings: bfloat16 [65536, 768], P('dp'), may hold values from -32 to 32
- centroids: bfloat16 [4096, 768], P('cent', 'dp'), may hold values from -4 to 4
Outputs:
- new_centroids: float32 [4096, 768], P('cent', 'dp')
All inputs are finite; a program needn't handle non-finite values.
Results may differ from a plain program's by a relative error of at most 0.002.
Values may be sent and summed in bfloat16 or wider, within the bound.
A program may use at most 64 MiB of HBM per device.

v0:
```python
import math

import jax
import jax.numpy as jnp
from jax import lax
from jax.sharding import PartitionSpec as P

ITERS = 2


def body(embeddings, centroids):
    local_cent = lax.all_gather(centroids, "dp", axis=1, tiled=True)
    rows, width = embeddings.shape
    cols = local_cent.shape[0]
    total_rows = rows * lax.axis_size("dp")
    total_cols = cols * lax.axis_size("cent")
    scale = 4.0 / math.sqrt(width)
    step_rows = math.gcd(rows, 512)
    count = rows // step_rows
    pieces = embeddings.reshape(count, step_rows, width)

    def logits_of(piece):
        return (
            lax.dot_general(
                piece, local_cent, (((1,), (1,)), ((), ())), preferred_element_type=jnp.float32
            )
            * scale
        )

    def row_pass(col_pot):

        def local_stats(piece):
            shifted = logits_of(piece) + col_pot[None, :]
            top = jnp.max(shifted, axis=1)
            return (top, jnp.sum(jnp.exp(shifted - top[:, None]), axis=1))

        tops, totals = lax.map(local_stats, pieces)
        tops = tops.reshape(rows)
        totals = totals.reshape(rows)
        peak = lax.pmax(tops, "cent")
        whole = lax.psum(totals * jnp.exp(tops - peak), "cent")
        return (-(peak + jnp.log(whole))).reshape(count, step_rows)

    def col_pass(row_pot):

        def one(carry, item):
            piece, pots = item
            shifted = logits_of(piece) + pots[:, None]
            peak, acc = carry
            new_peak = jnp.maximum(peak, jnp.max(shifted, axis=0))
            acc = acc * jnp.exp(peak - new_peak) + jnp.sum(
                jnp.exp(shifted - new_peak[None, :]), axis=0
            )
            return ((new_peak, acc), None)

        init = (jnp.full((cols,), -1e30, jnp.float32), jnp.zeros((cols,), jnp.float32))
        (tops, totals), _ = lax.scan(one, init, (pieces, row_pot))
        peak = lax.pmax(tops, "dp")
        whole = lax.psum(totals * jnp.exp(tops - peak), "dp")
        return jnp.log(jnp.float32(total_rows) / total_cols) - (peak + jnp.log(whole))

    col_pot = jnp.zeros((cols,), jnp.float32)
    for step in range(ITERS):
        row_pot = row_pass(col_pot)
        col_pot = col_pass(row_pot)
    row_pot = row_pass(col_pot)

    def final(carry, item):
        piece, pots = item
        plan = jnp.exp(logits_of(piece) + pots[:, None] + col_pot[None, :])
        sums, mass = carry
        mass = mass + jnp.sum(plan, axis=0)
        sums = sums + lax.dot_general(
            plan.astype(jnp.bfloat16),
            piece,
            (((0,), (0,)), ((), ())),
            preferred_element_type=jnp.float32,
        )
        return ((sums, mass), None)

    init = (jnp.zeros((cols, width), jnp.float32), jnp.zeros((cols,), jnp.float32))
    (sums, mass), _ = lax.scan(final, init, (pieces, row_pot))
    owned = lax.psum_scatter(sums, "dp", scatter_dimension=1, tiled=True)
    weight = lax.psum(mass, "dp")
    return owned / weight[:, None]


def solution(mesh):
    return jax.shard_map(
        body,
        mesh=mesh,
        in_specs=(P("dp", None), P("cent", "dp")),
        out_specs=P("cent", "dp"),
        check_vma=False,
    )
```

profile of v0, /device:TPU:0, one launch (start us, length us, event | category | flops | bytes accessed | tf_op | source)
XLA Modules:
  0.0 514.1 jit_solution(3372564652467690739)
XLA Ops:
  6.5 26.0 %all_gather.3 = bf16[512,768]{0,1:T(8,128)(2,1)S(1)} all-gather(bf16[512,48]{0,1:T(8,128)(2,1)} %param.15), channel_id=1, replica_groups=mesh['dp'=16,'cent'=8] {'dp'}, dimensions={1}, use_global_device_ids=true | all-gather | bytes 835584 | tf_op jit(solution)/shard_map/all_gather | solution.py:12
  32.8 16.8 %while.75 = (s32[]{:T(128)}, f32[8,512]{1,0:T(8,128)S(1)}, f32[8,512]{1,0:T(8,128)S(1)}, bf16[8,512,768]{2,1,0:T(8,128)(2,1)}, bf16[512,768]{1,0:T(8,128)(2,1)S(1)}, /*index=5*/s32[]{:T(128)}, s32[]{:T(128)}) while((s32[]{:T(128)}, f32[8,512]{1,0:T(8,128)S(1)}, f32[8,512]{1,0:T(8,128)S(1)}, bf16[8,512,768]{2,1,0:T(8,128)(2,1)}, ...), condition=%wide.region_3.4_spmd, body=%wide.region_0.3_spmd.sunk | while | flops 403700736 | bytes 3684449 | solution.py:37
  34.9 1.8 fusion.61
  37.0 1.8 fusion.61
  49.6 23.6 %pmax.35 = f32[4096]{0:T(1024)S(1)} all-reduce(f32[4096]{0:T(1024)S(1)} %bitcast.114), channel_id=1, replica_groups=mesh['dp'=16,'cent'=8] {'cent'}, use_global_device_ids=true, to_apply=%region_4.5 | all-reduce | flops 4096 | bytes 32768 | tf_op jit(solution)/shard_map/pmax | solution.py:40
  73.2 23.6 %psum.42 = f32[4096]{0:T(1024)S(1)} all-reduce(f32[4096]{0:T(1024)S(1)} %exponential_multiply_fusion.2), channel_id=1, replica_groups=mesh['dp'=16,'cent'=8] {'cent'}, use_global_device_ids=true, to_apply=%region_5.6 | all-reduce | flops 4096 | bytes 32768 | tf_op jit(solution)/shard_map/psum | solution.py:41
  96.8 16.2 %while.78 = (s32[]{:T(128)}, f32[512]{0:T(512)S(1)}, f32[512]{0:T(512)S(1)}, bf16[8,512,768]{2,1,0:T(8,128)(2,1)}, bf16[512,768]{1,0:T(8,128)(2,1)S(1)}, /*index=5*/f32[8,512]{1,0:T(8,128)S(1)}, s32[]{:T(128)}, s32[]{:T(128)}) while((s32[]{:T(128)}, f32[512]{0:T(512)S(1)}, f32[512]{0:T(512)S(1)}, bf16[8,512,768]{2,1,0:T(8,128)(2,1)}, ...), condition=%wide.region_9.10_spmd.clone, body=%wide.region_6.9_spmd.clone.sunk | while | flops 403966464 | bytes 3702896 | solution.py:57
  96.8 1.8 fusion.67
  98.8 1.8 fusion.67
  100.9 1.8 fusion.67
  102.9 1.8 fusion.67
  104.9 1.8 fusion.67
  106.9 1.8 fusion.67
  108.9 1.8 fusion.67
  111.0 1.8 fusion.67
  113.0 38.1 %pmax.36 = f32[512]{0:T(512)S(1)} all-reduce(f32[512]{0:T(512)S(1)} %get-tuple-element.205), channel_id=1, replica_groups=mesh['dp'=16,'cent'=8] {'dp'}, use_global_device_ids=true, to_apply=%region_10.11 | all-reduce | flops 512 | bytes 4096 | tf_op jit(solution)/shard_map/pmax | solution.py:58
  151.1 35.5 %psum.43 = f32[512]{0:T(512)S(1)} all-reduce(f32[512]{0:T(512)S(1)} %exponential_multiply_fusion.4), channel_id=1, replica_groups=mesh['dp'=16,'cent'=8] {'dp'}, use_global_device_ids=true, to_apply=%region_11.12 | all-reduce | flops 512 | bytes 4096 | tf_op jit(solution)/shard_map/psum | solution.py:59
  186.6 16.8 %while.76 = (s32[]{:T(128)}, f32[8,512]{1,0:T(8,128)S(1)}, f32[8,512]{1,0:T(8,128)S(1)}, bf16[8,512,768]{2,1,0:T(8,128)(2,1)}, bf16[512,768]{1,0:T(8,128)(2,1)S(1)}, /*index=5*/f32[512]{0:T(512)S(1)}, s32[]{:T(128)}, s32[]{:T(128)}) while((s32[]{:T(128)}, f32[8,512]{1,0:T(8,128)S(1)}, f32[8,512]{1,0:T(8,128)S(1)}, ...), condition=%wide.region_15.16_spmd, body=%wide.region_12.15_spmd.sunk | while | flops 403962880 | bytes 3686505 | solution.py:37
  186.6 1.8 fusion.63
  188.7 1.8 fusion.63
  190.8 1.8 fusion.63
  195.0 1.8 fusion.63
  197.1 1.8 fusion.63
  199.2 1.8 fusion.63
  203.4 23.6 %pmax.37 = f32[4096]{0:T(1024)S(1)} all-reduce(f32[4096]{0:T(1024)S(1)} %bitcast.116), channel_id=1, replica_groups=mesh['dp'=16,'cent'=8] {'cent'}, use_global_device_ids=true, to_apply=%region_16.17 | all-reduce | flops 4096 | bytes 32768 | tf_op jit(solution)/shard_map/pmax | solution.py:40
  227.0 23.6 %psum.44 = f32[4096]{0:T(1024)S(1)} all-reduce(f32[4096]{0:T(1024)S(1)} %exponential_multiply_fusion.1), channel_id=1, replica_groups=mesh['dp'=16,'cent'=8] {'cent'}, use_global_device_ids=true, to_apply=%region_17.18 | all-reduce | flops 4096 | bytes 32768 | tf_op jit(solution)/shard_map/psum | solution.py:41
  250.6 16.2 %while.79 = (s32[]{:T(128)}, f32[512]{0:T(512)S(1)}, f32[512]{0:T(512)S(1)}, bf16[8,512,768]{2,1,0:T(8,128)(2,1)}, bf16[512,768]{1,0:T(8,128)(2,1)S(1)}, /*index=5*/f32[8,512]{1,0:T(8,128)S(1)}, s32[]{:T(128)}, s32[]{:T(128)}) while((s32[]{:T(128)}, f32[512]{0:T(512)S(1)}, f32[512]{0:T(512)S(1)}, ...), condition=%wide.region_21.22_spmd.clone, body=%wide.region_18.21_spmd.clone.sunk | while | flops 403966464 | bytes 3702896 | solution.py:57
  250.6 1.8 fusion.70
  252.6 1.8 fusion.70
  254.6 1.8 fusion.70
  256.6 1.8 fusion.70
  258.7 1.8 fusion.70
  260.7 1.8 fusion.70
  262.7 1.8 fusion.70
  264.7 1.8 fusion.70
  266.7 37.5 %pmax.38 = f32[512]{0:T(512)S(1)} all-reduce(f32[512]{0:T(512)S(1)} %get-tuple-element.209), channel_id=1, replica_groups=mesh['dp'=16,'cent'=8] {'dp'}, use_global_device_ids=true, to_apply=%region_22.23 | all-reduce | flops 512 | bytes 4096 | tf_op jit(solution)/shard_map/pmax | solution.py:58
  304.2 35.5 %psum.45 = f32[512]{0:T(512)S(1)} all-reduce(f32[512]{0:T(512)S(1)} %exponential_multiply_fusion.3), channel_id=1, replica_groups=mesh['dp'=16,'cent'=8] {'dp'}, use_global_device_ids=true, to_apply=%region_23.24 | all-reduce | flops 512 | bytes 4096 | tf_op jit(solution)/shard_map/psum | solution.py:59
  339.7 16.8 %while.77 = (s32[]{:T(128)}, f32[8,512]{1,0:T(8,128)S(1)}, f32[8,512]{1,0:T(8,128)S(1)}, bf16[8,512,768]{2,1,0:T(8,128)(2,1)}, bf16[512,768]{1,0:T(8,128)(2,1)S(1)}, /*index=5*/f32[512]{0:T(512)S(1)}, s32[]{:T(128)}, s32[]{:T(128)}) while((s32[]{:T(128)}, f32[8,512]{1,0:T(8,128)S(1)}, f32[8,512]{1,0:T(8,128)S(1)}, ...), condition=%wide.region_27.28_spmd, body=%wide.region_24.27_spmd.sunk | while | flops 403962880 | bytes 3686505 | solution.py:37
  339.7 1.8 fusion.65
  341.8 1.8 fusion.65
  343.9 1.8 fusion.65
  346.0 1.8 fusion.65
  348.1 1.8 fusion.65
  356.5 23.6 %pmax.39 = f32[4096]{0:T(1024)S(1)} all-reduce(f32[4096]{0:T(1024)S(1)} %bitcast.118), channel_id=1, replica_groups=mesh['dp'=16,'cent'=8] {'cent'}, use_global_device_ids=true, to_apply=%region_28.29 | all-reduce | flops 4096 | bytes 32768 | tf_op jit(solution)/shard_map/pmax | solution.py:40
  380.1 23.6 %psum.46 = f32[4096]{0:T(1024)S(1)} all-reduce(f32[4096]{0:T(1024)S(1)} %exponential_multiply_fusion), channel_id=1, replica_groups=mesh['dp'=16,'cent'=8] {'cent'}, use_global_device_ids=true, to_apply=%region_29.30 | all-reduce | flops 4096 | bytes 32768 | tf_op jit(solution)/shard_map/psum | solution.py:41
  403.6 31.2 %while.80 = (s32[]{:T(128)}, f32[512,768]{1,0:T(8,128)S(1)}, f32[512]{0:T(512)S(1)}, bf16[8,512,768]{2,1,0:T(8,128)(2,1)}, bf16[512,768]{1,0:T(8,128)(2,1)S(1)},...) while((s32[]{:T(128)}, f32[512,768]{1,0:T(8,128)S(1)}, ...), condition=%wide.region_32.33_spmd.clone, body=%wide.region_30.32_spmd.clone.sunk | while | flops 807404032 | bytes 6570108 | solution.py:82
  403.7 1.8 fusion.75
  405.5 2.0 select_add_fusion.4
  407.6 1.8 fusion.75
  409.4 2.0 select_add_fusion.4
  411.5 1.8 fusion.75
  413.4 2.0 select_add_fusion.4
  415.4 1.8 fusion.75
  417.2 2.0 select_add_fusion.4
  419.3 1.8 fusion.75
  421.1 2.0 select_add_fusion.4
  423.2 1.8 fusion.75
  425.0 2.0 select_add_fusion.4
  427.1 1.8 fusion.75
  428.9 2.0 select_add_fusion.4
  431.0 1.8 fusion.75
  432.8 2.0 select_add_fusion.4
  436.5 37.6 %psum.47 = f32[512]{0:T(512)S(1)} all-reduce(f32[512]{0:T(512)S(1)} %get-tuple-element.214), channel_id=1, replica_groups=mesh['dp'=16,'cent'=8] {'dp'}, use_global_device_ids=true, to_apply=%region_34.35 | all-reduce | flops 512 | bytes 4096 | tf_op jit(solution)/shard_map/psum | solution.py:84
  474.1 31.7 %reduce-scatter.2.cloned.1.call-done = f32[512,48]{0,1:T(8,128)} async-done(((f32[512,768]{0,1:T(8,128)}), f32[512,48]{0,1:T(8,128)}) %reduce-scatter.2.cloned.1.call-update) | async-done | bytes 98320 | tf_op jit(solution)/shard_map/reduce_scatter | solution.py:83
  (215 shorter events, 34.3 us)
Async XLA Ops:
  6.5 499.2 %reduce-scatter.2.cloned.1.call-start = ((), (), s32[]{:S(2)}) async-start(), calls=%async_computation.1 | async-start | bytes 1671168 | tf_op jit(solution)/shard_map/reduce_scatter | solution.py:83
Sparse Core Ops, SparseCore 0:
  436.6 69.0 reduce-scatter.1
where the time goes:
time: 517 us; the launch traced here: 514 us
  blocking collectives  351 us (68%)
  matrix products  101 us (20%)
  waiting for transfers between devices  31.7 us (6%)
  between operations  13.5 us (3%)
  other arithmetic  9.97 us (2%)
    dot_general x48, matrix products, logits_of(): lax.dot_general(piece, local_cent, (((1,), (1,)), ((), ())), preferred_el...  84.9 us
    pmax x2, blocking collectives, col_pass(): peak = lax.pmax(tops, 'dp')  75.6 us
    psum x2, blocking collectives, col_pass(): whole = lax.psum(totals * jnp.exp(tops - peak), 'dp')  70.9 us
    psum x3, blocking collectives, row_pass(): whole = lax.psum(totals * jnp.exp(tops - peak), 'cent')  70.7 us
    pmax x3, blocking collectives, row_pass(): peak = lax.pmax(tops, 'cent')  70.7 us
    psum x1, blocking collectives, body(): weight = lax.psum(mass, 'dp')  37.6 us
    reduce_scatter x1, waiting for transfers between devices, body(): owned = lax.psum_scatter(sums, 'dp', scatter_dimension=1, tiled=True)  31.7 us
    all_gather x1, blocking collectives, body(): local_cent = lax.all_gather(centroids, 'dp', axis=1, tiled=True)  26 us
  transfers between devices with their start and end apart: 1, of which 1 were waited for; matrix products, arithmetic and copies ran while one was open for 0% of the time, Pallas kernels for 0%

commit v1 on v0

v1 whole, which is shorter than its diff:
```python
import functools
import math

import jax
import jax.numpy as jnp
from jax import lax
from jax.experimental import pallas as pl
from jax.experimental.pallas import tpu as pltpu
from jax.sharding import PartitionSpec as P

MESH = pl.DeviceIdType.MESH
f32 = jnp.float32
bf16 = jnp.bfloat16
LANES = 128
GROUP = 128
ROUNDS = 3
E_PARTS = 4
HALVES = 2


def nt_dot(a, b):
    return lax.dot_general(a, b, (((1,), (1,)), ((), ())), preferred_element_type=f32)


def nn_dot(a, b):
    return lax.dot_general(a, b, (((1,), (0,)), ((), ())), preferred_element_type=f32)


def lse2(parts):
    top = functools.reduce(jnp.maximum, parts)
    return top + jnp.log2(functools.reduce(jnp.add, [jnp.exp2(p - top) for p in parts]))


def to_lanes(col):
    return jnp.broadcast_to(col, (GROUP, LANES)).T[0:1, :]


def to_rows(row):
    return jnp.broadcast_to(row, (LANES, GROUP)).T


def kernel(
    ndp, ncent, chunks,
    e_hbm, c_ref, out_ref,
    e, ct_own, ct, c, b, plan, sums, low,
    row_own, row_in, acc8, pot,
    col_own, col_in, mass_own, mass_in,
    peak, fac, rs_in,
    e_sem, ct_send, ct_recv, row_send, row_recv, col_send, col_recv, mass_send, mass_recv, rs_send, rs_recv,
):
    n, width = e.shape
    k = c.shape[0]
    own = width // ndp
    ny = math.isqrt(ndp)
    nz = ndp // ny
    w = n // (8 * chunks)
    groups = k // GROUP
    half = k // HALVES
    total_ratio = math.log2((n * ndp) / (k * ncent))

    me = lax.axis_index("dp")
    mec = lax.axis_index("cent")
    my_z, my_y = me // ny, me % ny

    offsets = [(dz, dy) for dz in range(nz) for dy in range(ny)][1:]

    def dp_peer(dz, dy):
        return ((my_z + dz) % nz) * ny + (my_y + dy) % ny

    def cent_peer(o):
        return (mec + o) % ncent

    e_copies = []
    step = n // E_PARTS
    for i in range(E_PARTS):
        rows = pl.ds(i * step, step)
        e_copies.append(pltpu.make_async_copy(e_hbm.at[rows], e.at[rows], e_sem.at[i]))
        e_copies[-1].start()

    barrier = pltpu.get_barrier_semaphore()
    for dz, dy in offsets:
        pl.semaphore_signal(barrier, inc=1, device_id={"dp": dp_peer(dz, dy)}, device_id_type=MESH)
    for o in range(1, ncent):
        pl.semaphore_signal(barrier, inc=1, device_id={"cent": cent_peer(o)}, device_id_type=MESH)

    eye = (
        lax.broadcasted_iota(jnp.int32, (own, own), 0) == lax.broadcasted_iota(jnp.int32, (own, own), 1)
    ).astype(f32).astype(bf16)
    ct_own[...] = nt_dot(eye, c_ref[...]).astype(bf16)
    mine = pl.ds(pl.multiple_of(me * own, own), own)
    ct[mine, :] = ct_own[...]

    pl.semaphore_wait(barrier, len(offsets) + ncent - 1)

    for h in range(HALVES):
        cols = pl.ds(h * half, half)
        for dz, dy in offsets:
            pltpu.make_async_remote_copy(
                src_ref=ct_own.at[:, cols], dst_ref=ct.at[mine, cols],
                send_sem=ct_send.at[h], recv_sem=ct_recv.at[h],
                device_id={"dp": dp_peer(dz, dy)}, device_id_type=MESH,
            ).start()

    def wait_ct(sem, h):
        part = ct.at[pl.ds(0, own * (ndp - 1)), pl.ds(h * half, half)]
        pltpu.make_async_copy(part, part, sem.at[h]).wait()

    unit = 4.0 / math.sqrt(width) / math.log(2.0)
    wide = 2 * w

    def send_rows(r, ch):
        for o in range(1, ncent):
            pltpu.make_async_remote_copy(
                src_ref=row_own.at[r, ch], dst_ref=row_in.at[r, ch, o - 1],
                send_sem=row_send.at[r, ch], recv_sem=row_recv.at[r, ch],
                device_id={"cent": cent_peer(o)}, device_id_type=MESH,
            ).start()

    def wait_rows(sem, r, ch):
        part = row_in.at[r, ch]
        pltpu.make_async_copy(part, part, sem.at[r, ch]).wait()

    for h in range(HALVES):
        wait_ct(ct_recv, h)
        rows = pl.ds(h * half, half)
        c[rows, :] = ct[:, rows].T
        for ch in range(chunks):
            for i in range(0, 8, 2):
                at = (ch * 8 + i) * w
                toks = pl.ds(at, wide)
                if h == 0 and at % step == 0:
                    e_copies[at // step].wait()
                x = nt_dot(c[rows, :], e[toks, :]) * unit
                b[rows, toks] = x
                top = jnp.max(x, axis=0, keepdims=True)
                tot = jnp.sum(jnp.exp2(x - top), axis=0, keepdims=True)
                lse = top + jnp.log2(tot)
                if h == 0:
                    acc8[0:1, toks] = lse
                else:
                    lse = lse2([lse, acc8[0:1, toks]])
                    row_own[0, ch, i : i + 1, :] = lse[:, :w]
                    row_own[0, ch, i + 1 : i + 2, :] = lse[:, w:]
            if h == HALVES - 1:
                send_rows(0, ch)

    tiles = n // LANES
    per = w // LANES
    for ch in range(chunks):
        wait_rows(row_recv, 0, ch)
        dense = -lse2([row_own[0, ch]] + [row_in[0, ch, j] for j in range(ncent - 1)])
        for i in range(8):
            pot[0:1, pl.ds((ch * 8 + i) * w, w)] = dense[i : i + 1, :]

    def tile(i):
        return pl.ds(pl.multiple_of(i * LANES, LANES), LANES)

    def send_cols(r):
        for o, (dz, dy) in enumerate(offsets):
            pltpu.make_async_remote_copy(
                src_ref=col_own.at[r], dst_ref=col_in.at[r, o],
                send_sem=col_send.at[r], recv_sem=col_recv.at[r],
                device_id={"dp": dp_peer(dz, dy)}, device_id_type=MESH,
            ).start()

    def wait_cols(sem, r):
        part = col_in.at[r]
        pltpu.make_async_copy(part, part, sem.at[r]).wait()

    for g in range(groups):
        gs = pl.ds(g * GROUP, GROUP)

        def top_step(i, m):
            return jnp.maximum(m, b[gs, tile(i)] + pot[0:1, tile(i)])

        m = lax.fori_loop(0, tiles, top_step, jnp.full((GROUP, LANES), -jnp.inf, f32), unroll=4)
        m = jnp.broadcast_to(jnp.max(m, axis=1, keepdims=True), (GROUP, LANES))
        peak[gs, :] = m

        def exp_step(i, a):
            x = jnp.exp2((b[gs, tile(i)] + pot[0:1, tile(i)]) - m)
            b[gs, tile(i)] = x
            return a + x

        a = lax.fori_loop(0, tiles, exp_step, jnp.zeros((GROUP, LANES), f32), unroll=4)
        lse = m[:, 0:1] + jnp.log2(jnp.sum(a, axis=1, keepdims=True))
        col_own[0, g : g + 1, :] = to_lanes(lse)
    send_cols(0)
    wait_cols(col_recv, 0)
    lse = lse2([col_own[0]] + [col_in[0, j] for j in range(ndp - 1)])
    for g in range(groups):
        gs = pl.ds(g * GROUP, GROUP)
        fac[gs, :] = jnp.exp2((peak[gs, :] - to_rows(lse[g : g + 1, :])) + total_ratio)

    def row_pass(r):
        for g in range(groups):
            gs = pl.ds(g * GROUP, GROUP)
            f = fac[gs, :]

            def step_(i, _):
                x = jnp.sum((b[gs, tile(i)] * f).reshape(GROUP // 8, 8, LANES), axis=0)
                if g > 0:
                    x = x + acc8[:, tile(i)]
                acc8[:, tile(i)] = x
                return 0

            lax.fori_loop(0, tiles, step_, 0, unroll=4)
        for ch in range(chunks):
            for i in range(8):
                s = jnp.sum(acc8[:, pl.ds((ch * 8 + i) * w, w)], axis=0, keepdims=True)
                row_own[r, ch, i : i + 1, :] = s
            send_rows(r, ch)
        for ch in range(chunks):
            wait_rows(row_recv, r, ch)
            dense = row_own[r, ch]
            for j in range(ncent - 1):
                dense = dense + row_in[r, ch, j]
            dense = 1.0 / dense
            for i in range(8):
                pot[0:1, pl.ds((ch * 8 + i) * w, w)] = dense[i : i + 1, :]

    row_pass(1)

    for g in range(groups):
        gs = pl.ds(g * GROUP, GROUP)

        def col_step(i, a):
            return a + b[gs, tile(i)] * pot[0:1, tile(i)]

        a = lax.fori_loop(0, tiles, col_step, jnp.zeros((GROUP, LANES), f32), unroll=4)
        col_own[1, g : g + 1, :] = to_lanes(jnp.sum(a * fac[gs, :], axis=1, keepdims=True))
    send_cols(1)
    wait_cols(col_recv, 1)
    tot = col_own[1]
    for j in range(ndp - 1):
        tot = tot + col_in[1, j]
    tot = (2.0**total_ratio) / tot
    for g in range(groups):
        gs = pl.ds(g * GROUP, GROUP)
        fac[gs, :] = fac[gs, :] * to_rows(tot[g : g + 1, :])

    row_pass(2)

    for g in range(groups):
        gs = pl.ds(g * GROUP, GROUP)
        f = fac[gs, :]

        def plan_step(i, a):
            x = (b[gs, tile(i)] * f) * pot[0:1, tile(i)]
            plan[gs, tile(i)] = x.astype(bf16)
            return a + x

        a = lax.fori_loop(0, tiles, plan_step, jnp.zeros((GROUP, LANES), f32), unroll=4)
        mass_own[g : g + 1, :] = to_lanes(jnp.sum(a, axis=1, keepdims=True))
    for o, (dz, dy) in enumerate(offsets):
        pltpu.make_async_remote_copy(
            src_ref=mass_own, dst_ref=mass_in.at[o], send_sem=mass_send, recv_sem=mass_recv,
            device_id={"dp": dp_peer(dz, dy)}, device_id_type=MESH,
        ).start()

    blk = 256 if width % 256 == 0 else width
    for j in range(width // blk):
        feats = pl.ds(j * blk, blk)
        s = nn_dot(plan[...], e[:, feats]).T
        sums[feats, :] = s
        low[feats, :] = s.astype(bf16)
    for o, (dz, dy) in enumerate(offsets):
        peer = dp_peer(dz, dy)
        pltpu.make_async_remote_copy(
            src_ref=low.at[pl.ds(pl.multiple_of(peer * own, own), own), :], dst_ref=rs_in.at[o],
            send_sem=rs_send, recv_sem=rs_recv, device_id={"dp": peer}, device_id_type=MESH,
        ).start()

    pltpu.make_async_copy(mass_in, mass_in, mass_recv).wait()
    mass = mass_own[...]
    for j in range(ndp - 1):
        mass = mass + mass_in[j]
    pltpu.make_async_copy(rs_in, rs_in, rs_recv).wait()
    for g in range(groups):
        gs = pl.ds(g * GROUP, GROUP)
        tot = sums[mine, gs]
        for j in range(ndp - 1):
            tot = tot + rs_in[j, :, gs].astype(f32)
        out_ref[:, gs] = tot / mass[g : g + 1, :]

    for h in range(HALVES):
        wait_ct(ct_send, h)
    for r in range(ROUNDS):
        for ch in range(chunks):
            wait_rows(row_send, r, ch)
    for r in range(ROUNDS - 1):
        wait_cols(col_send, r)
    pltpu.make_async_copy(mass_in, mass_in, mass_send).wait()
    pltpu.make_async_copy(rs_in, rs_in, rs_send).wait()


def body(embeddings, centroids):
    ndp, ncent = lax.axis_size("dp"), lax.axis_size("cent")
    n, width = embeddings.shape
    k, own = centroids.shape
    chunks = 2
    w = n // (8 * chunks)
    dma = pltpu.SemaphoreType.DMA
    out = pl.pallas_call(
        functools.partial(kernel, ndp, ncent, chunks),
        out_shape=jax.ShapeDtypeStruct((own, k), f32),
        in_specs=[pl.BlockSpec(memory_space=pl.ANY), pl.BlockSpec(memory_space=pltpu.VMEM)],
        out_specs=pl.BlockSpec(memory_space=pltpu.VMEM),
        scratch_shapes=[
            pltpu.VMEM((n, width), bf16),
            pltpu.VMEM((own, k), bf16),
            pltpu.VMEM((width, k), bf16),
            pltpu.VMEM((k, width), bf16),
            pltpu.VMEM((k, n), f32),
            pltpu.VMEM((k, n), bf16),
            pltpu.VMEM((width, k), f32),
            pltpu.VMEM((width, k), bf16),
            pltpu.VMEM((ROUNDS, chunks, 8, w), f32),
            pltpu.VMEM((ROUNDS, chunks, ncent - 1, 8, w), f32),
            pltpu.VMEM((8, n), f32),
            pltpu.VMEM((8, n), f32),
            pltpu.VMEM((ROUNDS - 1, k // GROUP, LANES), f32),
            pltpu.VMEM((ROUNDS - 1, ndp - 1, k // GROUP, LANES), f32),
            pltpu.VMEM((k // GROUP, LANES), f32),
            pltpu.VMEM((ndp - 1, k // GROUP, LANES), f32),
            pltpu.VMEM((k, LANES), f32),
            pltpu.VMEM((k, LANES), f32),
            pltpu.VMEM((ndp - 1, own, k), bf16),
            dma((E_PARTS,)),
            dma((HALVES,)),
            dma((HALVES,)),
            dma((ROUNDS, chunks)),
            dma((ROUNDS, chunks)),
            dma((ROUNDS - 1,)),
            dma((ROUNDS - 1,)),
            dma,
            dma,
            dma,
            dma,
        ],
        compiler_params=pltpu.CompilerParams(
            collective_id=0, has_side_effects=True, vmem_limit_bytes=60 * 2**20
        ),
        name="sinkhorn",
    )(embeddings, centroids)
    return out.T


def solution(mesh):
    return jax.shard_map(
        body,
        mesh=mesh,
        in_specs=(P("dp", None), P("cent", "dp")),
        out_specs=P("cent", "dp"),
        check_vma=False,
    )
```

time: 517 us -> 76 us (0.15)
  blocking collectives: 351 us -> 0 us
  matrix products: 101 us -> 0 us
  Pallas kernels: 0 us -> 72.5 us
  waiting for transfers between devices: 31.7 us -> 0 us
  between operations: 13.5 us -> 0.01 us
  other arithmetic: 9.97 us -> 0 us
    psum x6 -> x0, blocking collectives: 179 us -> none  [the longest x2 70.9 us: col_pass(): whole = lax.psum(totals * jnp.exp(tops - peak), 'dp')]
    pmax x5 -> x0, blocking collectives: 146 us -> none  [the longest x2 75.6 us: col_pass(): peak = lax.pmax(tops, 'dp')]
    dot_general x56 -> x0, matrix products: 101 us -> none  [the longest x48 84.9 us: logits_of(): lax.dot_general(piece, local_cent, (((1,), (1,)), ((), ())), preferred_el...]
    pallas_call x0 -> x1, Pallas kernels: none -> 72.5 us  [body(): pl.pallas_call(functools.partial(kernel, ndp, ncent, chunks), out_shape=j...]
    reduce_scatter x1 -> x0, waiting for transfers between devices: 31.7 us -> none  [body(): owned = lax.psum_scatter(sums, 'dp', scatter_dimension=1, tiled=True)]
    all_gather x1 -> x0, blocking collectives: 26 us -> none  [body(): local_cent = lax.all_gather(centroids, 'dp', axis=1, tiled=True)]
    reduce_sum x40 -> x0, other arithmetic: 7.86 us -> none  [the longest x24 4.72 us: local_stats(): return (top, jnp.sum(jnp.exp(shifted - top[:, None]), axis=1))]
  transfers between devices with their start and end apart: 1 -> 0, of which waited for: 1 -> 0; matrix products, arithmetic and copies ran while one was open for 0% -> 0% of each run, Pallas kernels for 0% -> 0%
where the time goes in v1:
time: 76 us; the launch traced here: 75.6 us
  Pallas kernels  72.5 us (95%)
  local copies, waits for them, and re-layouts  3.08 us (4%)
    pallas_call x1, Pallas kernels, body(): pl.pallas_call(functools.partial(kernel, ndp, ncent, chunks), out_shape=j...  72.5 us
    unnamed x2, local copies, waits for them, and re-layouts  3.08 us

profile of v1, /device:TPU:0, one launch (start us, length us, event | category | flops | bytes accessed | tf_op | source)
XLA Modules:
  0.0 75.6 jit_solution(12566830582335611567)
XLA Ops:
  0.0 1.5 %copy.3.c_ref = bf16[512,48]{1,0:T(8,128)(2,1)} copy(bf16[512,48]{0,1:T(8,128)(2,1)} %param.3) | data formatting | bytes 98304 | tf_op args[1]
  1.5 72.5 %sinkhorn.1 = f32[48,512]{1,0:T(8,128)} custom-call(bf16[4096,768]{1,0:T(8,128)(2,1)} %e_hbm.1, bf16[512,48]{1,0:T(8,128)(2,1)} %copy.3.c_ref), custom_call_target="tpu_custom_call" | custom-call | tf_op jit(solution)/shard_map/sinkhorn/pallas_call | solution.py:304
  74.1 1.5 %copy.5 = f32[512,48]{0,1:T(8,128)} copy(f32[512,48]{0,1:T(8,128)} %bitcast.1) | data formatting | bytes 196608

commit v2 on v1

v2 whole, which is shorter than its diff:
```python
import functools
import math

import jax
import jax.numpy as jnp
from jax import lax
from jax.experimental import pallas as pl
from jax.experimental.pallas import tpu as pltpu
from jax.sharding import PartitionSpec as P

MESH = pl.DeviceIdType.MESH
f32 = jnp.float32
bf16 = jnp.bfloat16
LANES = 128
GROUP = 128
ROUNDS = 3
E_PARTS = 4
HALVES = 2


def nt_dot(a, b):
    return lax.dot_general(a, b, (((1,), (1,)), ((), ())), preferred_element_type=f32)


def nn_dot(a, b):
    return lax.dot_general(a, b, (((1,), (0,)), ((), ())), preferred_element_type=f32)


def lse2(parts):
    top = functools.reduce(jnp.maximum, parts)
    return top + jnp.log2(functools.reduce(jnp.add, [jnp.exp2(p - top) for p in parts]))


def to_lanes(col):
    return jnp.broadcast_to(col, (GROUP, LANES)).T[0:1, :]


def to_rows(row):
    return jnp.broadcast_to(row, (LANES, GROUP)).T


def kernel(
    ndp, ncent, chunks,
    e_hbm, c_hbm, out_ref,
    c_in, e, ct_own, ct, c, b, plan, sums, low,
    row_own, row_in, acc8, pot,
    col_own, col_in, mass_own, mass_in,
    peak, fac, part, rs_in,
    c_sem, e_sem, near_recv, ct_send, ct_recv, row_send, row_recv, col_send, col_recv,
    mass_send, mass_recv, rs_send, rs_recv,
):
    n, width = e.shape
    k = c.shape[0]
    own = width // ndp
    ny = math.isqrt(ndp)
    nz = ndp // ny
    w = n // (8 * chunks)
    groups = k // GROUP
    half = k // HALVES
    total_ratio = math.log2((n * ndp) / (k * ncent))

    pending = []

    me = lax.axis_index("dp")
    mec = lax.axis_index("cent")
    my_z, my_y = me // ny, me % ny

    offsets = [(dz, dy) for dz in range(nz) for dy in range(ny)][1:]

    def dp_peer(dz, dy):
        return ((my_z + dz) % nz) * ny + (my_y + dy) % ny

    def cent_peer(o):
        return (mec + o) % ncent

    barrier = pltpu.get_barrier_semaphore()
    for dz, dy in offsets:
        pl.semaphore_signal(barrier, inc=1, device_id={"dp": dp_peer(dz, dy)}, device_id_type=MESH)
    for o in range(1, ncent):
        pl.semaphore_signal(barrier, inc=1, device_id={"cent": cent_peer(o)}, device_id_type=MESH)

    c_copy = pltpu.make_async_copy(c_hbm, c_in, c_sem)
    c_copy.start()
    e_copies = []
    step = n // E_PARTS
    for i in range(E_PARTS):
        rows = pl.ds(i * step, step)
        e_copies.append(pltpu.make_async_copy(e_hbm.at[rows], e.at[rows], e_sem.at[i]))
        e_copies[-1].start()

    eye = (
        lax.broadcasted_iota(jnp.int32, (own, own), 0) == lax.broadcasted_iota(jnp.int32, (own, own), 1)
    ).astype(f32).astype(bf16)
    c_copy.wait()
    ct_own[...] = nt_dot(eye, c_in[...]).astype(bf16)

    def feats_of(dp):
        return pl.ds(pl.multiple_of(dp * own, own), own)

    mine = feats_of(me)
    ct[mine, :] = ct_own[...]

    pl.semaphore_wait(barrier, len(offsets) + ncent - 1)

    quarters = 2 * HALVES
    quart = k // quarters

    def line(q, first):
        if (q % 2 == 0) == first:
            return [(d, 0) for d in range(1, nz)]
        return [(0, d) for d in range(1, ny)]

    def send_ct(q, src, rows, off, sem):
        cols = pl.ds(q * quart, quart)
        pltpu.make_async_remote_copy(
            src_ref=src.at[:, cols] if src is ct_own else src.at[rows, cols], dst_ref=ct.at[rows, cols],
            send_sem=ct_send.at[q], recv_sem=sem,
            device_id={"dp": dp_peer(*off)}, device_id_type=MESH,
        ).start()

    def wait_ct(sem, q, blocks):
        part_ = ct.at[pl.ds(0, own * blocks), pl.ds(q * quart, quart)]
        pltpu.make_async_copy(part_, part_, sem).wait()

    for q in range(quarters):
        for j, off in enumerate(line(q, True)):
            send_ct(q, ct_own, mine, off, near_recv.at[q, j])
        for off in line(q, False):
            send_ct(q, ct_own, mine, off, ct_recv.at[q])
        pending.append(functools.partial(wait_ct, ct_send.at[q], q, ndp - 1))
    for q in range(quarters):
        near = line(q, True)
        order = sorted(range(len(near)), key=lambda j: min(j + 1, len(near) - j))
        for j in order:
            wait_ct(near_recv.at[q, len(near) - 1 - j], q, 1)
            for off in line(q, False):
                send_ct(q, ct, feats_of(dp_peer(*near[j])), off, ct_recv.at[q])

    unit = 4.0 / math.sqrt(width) / math.log(2.0)
    wide = 2 * w

    def send_rows(r, ch):
        for o in range(1, ncent):
            pltpu.make_async_remote_copy(
                src_ref=row_own.at[r, ch], dst_ref=row_in.at[r, ch, o - 1],
                send_sem=row_send.at[r, ch], recv_sem=row_recv.at[r, ch],
                device_id={"cent": cent_peer(o)}, device_id_type=MESH,
            ).start()
        pending.append(lambda: wait_rows(row_send, r, ch))

    def wait_rows(sem, r, ch):
        part_ = row_in.at[r, ch]
        pltpu.make_async_copy(part_, part_, sem.at[r, ch]).wait()

    for h in range(HALVES):
        for q in (2 * h, 2 * h + 1):
            wait_ct(ct_recv.at[q], q, ndp - 1 - len(line(q, True)))
        rows = pl.ds(h * half, half)
        c[rows, :] = ct[:, rows].T
        for ch in range(chunks):
            for i in range(0, 8, 2):
                at = (ch * 8 + i) * w
                toks = pl.ds(at, wide)
                if h == 0 and at % step == 0:
                    e_copies[at // step].wait()
                x = nt_dot(c[rows, :], e[toks, :]) * unit
                b[rows, toks] = x
                top = jnp.max(x, axis=0, keepdims=True)
                tot = jnp.sum(jnp.exp2(x - top), axis=0, keepdims=True)
                lse = top + jnp.log2(tot)
                if h == 0:
                    acc8[0:1, toks] = lse
                else:
                    lse = lse2([lse, acc8[0:1, toks]])
                    row_own[0, ch, i : i + 1, :] = lse[:, :w]
                    row_own[0, ch, i + 1 : i + 2, :] = lse[:, w:]
            if h == HALVES - 1:
                send_rows(0, ch)

    tiles = n // (chunks * LANES)

    def tile(ch, i):
        return pl.ds(pl.multiple_of((ch * tiles + i) * LANES, LANES), LANES)

    def over_tiles(f, init):
        return lax.fori_loop(0, tiles, f, init, unroll=tiles)

    def spread_rows(ch, dense):
        for i in range(8):
            pot[0:1, pl.ds((ch * 8 + i) * w, w)] = dense[i : i + 1, :]

    def send_cols(r):
        for o, (dz, dy) in enumerate(offsets):
            pltpu.make_async_remote_copy(
                src_ref=col_own.at[r], dst_ref=col_in.at[r, o],
                send_sem=col_send.at[r], recv_sem=col_recv.at[r],
                device_id={"dp": dp_peer(dz, dy)}, device_id_type=MESH,
            ).start()
        pending.append(lambda: wait_cols(col_send, r))

    def wait_cols(sem, r):
        part_ = col_in.at[r]
        pltpu.make_async_copy(part_, part_, sem.at[r]).wait()

    for ch in range(chunks):
        wait_rows(row_recv, 0, ch)
        spread_rows(ch, -lse2([row_own[0, ch]] + [row_in[0, ch, j] for j in range(ncent - 1)]))
        for g in range(groups):
            gs = pl.ds(g * GROUP, GROUP)

            def top_step(i, m):
                return jnp.maximum(m, b[gs, tile(ch, i)] + pot[0:1, tile(ch, i)])

            m = over_tiles(top_step, jnp.full((GROUP, LANES), -jnp.inf, f32))
            m = jnp.broadcast_to(jnp.max(m, axis=1, keepdims=True), (GROUP, LANES))
            peak[ch, gs, :] = m

            def exp_step(i, a):
                x = jnp.exp2((b[gs, tile(ch, i)] + pot[0:1, tile(ch, i)]) - m)
                b[gs, tile(ch, i)] = x
                return a + x

            a = over_tiles(exp_step, jnp.zeros((GROUP, LANES), f32))
            lse = to_lanes(m[:, 0:1] + jnp.log2(jnp.sum(a, axis=1, keepdims=True)))
            if ch > 0:
                lse = lse2([lse, col_own[0, g : g + 1, :]])
            col_own[0, g : g + 1, :] = lse
    send_cols(0)
    wait_cols(col_recv, 0)
    lse = lse2([col_own[0]] + [col_in[0, j] for j in range(ndp - 1)])
    for g in range(groups):
        gs = pl.ds(g * GROUP, GROUP)
        shift = total_ratio - to_rows(lse[g : g + 1, :])
        for ch in range(chunks):
            fac[ch, gs, :] = jnp.exp2(peak[ch, gs, :] + shift)

    def send_row_sums(r):
        for ch in range(chunks):
            for g in range(groups):
                gs = pl.ds(g * GROUP, GROUP)
                f = fac[ch, gs, :]

                def step_(i, _):
                    x = jnp.sum((b[gs, tile(ch, i)] * f).reshape(GROUP // 8, 8, LANES), axis=0)
                    if g > 0:
                        x = x + acc8[:, tile(ch, i)]
                    acc8[:, tile(ch, i)] = x
                    return 0

                over_tiles(step_, 0)
            for i in range(8):
                s = jnp.sum(acc8[:, pl.ds((ch * 8 + i) * w, w)], axis=0, keepdims=True)
                row_own[r, ch, i : i + 1, :] = s
            send_rows(r, ch)

    def take_row_sums(r, ch):
        wait_rows(row_recv, r, ch)
        dense = row_own[r, ch]
        for j in range(ncent - 1):
            dense = dense + row_in[r, ch, j]
        spread_rows(ch, 1.0 / dense)

    send_row_sums(1)
    for ch in range(chunks):
        take_row_sums(1, ch)
        for g in range(groups):
            gs = pl.ds(g * GROUP, GROUP)

            def col_step(i, a):
                return a + b[gs, tile(ch, i)] * pot[0:1, tile(ch, i)]

            a = over_tiles(col_step, jnp.zeros((GROUP, LANES), f32)) * fac[ch, gs, :]
            if ch > 0:
                a = a + part[gs, :]
            if ch < chunks - 1:
                part[gs, :] = a
            else:
                col_own[1, g : g + 1, :] = to_lanes(jnp.sum(a, axis=1, keepdims=True))
    send_cols(1)
    wait_cols(col_recv, 1)
    tot = col_own[1]
    for j in range(ndp - 1):
        tot = tot + col_in[1, j]
    tot = (2.0**total_ratio) / tot
    for g in range(groups):
        gs = pl.ds(g * GROUP, GROUP)
        scale = to_rows(tot[g : g + 1, :])
        for ch in range(chunks):
            fac[ch, gs, :] = fac[ch, gs, :] * scale

    send_row_sums(2)
    for ch in range(chunks):
        take_row_sums(2, ch)

    def make_plan(g):
        gs = pl.ds(g * GROUP, GROUP)
        a = jnp.zeros((GROUP, LANES), f32)
        for ch in range(chunks):
            f = fac[ch, gs, :]

            def plan_step(i, a):
                x = (b[gs, tile(ch, i)] * f) * pot[0:1, tile(ch, i)]
                plan[gs, tile(ch, i)] = x.astype(bf16)
                return a + x

            a = over_tiles(plan_step, a)
        mass_own[g : g + 1, :] = to_lanes(jnp.sum(a, axis=1, keepdims=True))

    def wait_sums(sem, g):
        part_ = rs_in.at[g]
        pltpu.make_async_copy(part_, part_, sem.at[g]).wait()

    make_plan(0)
    for g in range(groups):
        if g + 1 < groups:
            make_plan(g + 1)
        s = nn_dot(plan[pl.ds(g * GROUP, GROUP), :], e[...]).T
        sums[g] = s
        low[g] = s.astype(bf16)
        for o, (dz, dy) in enumerate(offsets):
            peer = dp_peer(dz, dy)
            pltpu.make_async_remote_copy(
                src_ref=low.at[g, feats_of(peer), :], dst_ref=rs_in.at[g, o],
                send_sem=rs_send.at[g], recv_sem=rs_recv.at[g],
                device_id={"dp": peer}, device_id_type=MESH,
            ).start()
        pending.append(functools.partial(wait_sums, rs_send, g))
        if g == max(groups - 2, 0):
            for o, (dz, dy) in enumerate(offsets):
                pltpu.make_async_remote_copy(
                    src_ref=mass_own, dst_ref=mass_in.at[o], send_sem=mass_send, recv_sem=mass_recv,
                    device_id={"dp": dp_peer(dz, dy)}, device_id_type=MESH,
                ).start()
            pending.append(lambda: pltpu.make_async_copy(mass_in, mass_in, mass_send).wait())

    pltpu.make_async_copy(mass_in, mass_in, mass_recv).wait()
    mass = mass_own[...]
    for j in range(ndp - 1):
        mass = mass + mass_in[j]
    for g in range(groups):
        wait_sums(rs_recv, g)
        tot = sums[g, mine, :]
        for j in range(ndp - 1):
            tot = tot + rs_in[g, j].astype(f32)
        out_ref[:, pl.ds(g * GROUP, GROUP)] = tot / mass[g : g + 1, :]

    for wait in pending:
        wait()


def body(embeddings, centroids):
    ndp, ncent = lax.axis_size("dp"), lax.axis_size("cent")
    n, width = embeddings.shape
    k, own = centroids.shape
    chunks = 2
    w = n // (8 * chunks)
    groups = k // GROUP
    line = math.isqrt(ndp)
    dma = pltpu.SemaphoreType.DMA
    out = pl.pallas_call(
        functools.partial(kernel, ndp, ncent, chunks),
        out_shape=jax.ShapeDtypeStruct((own, k), f32),
        in_specs=[pl.BlockSpec(memory_space=pl.ANY), pl.BlockSpec(memory_space=pl.ANY)],
        out_specs=pl.BlockSpec(memory_space=pltpu.VMEM),
        scratch_shapes=[
            pltpu.VMEM((k, own), bf16),
            pltpu.VMEM((n, width), bf16),
            pltpu.VMEM((own, k), bf16),
            pltpu.VMEM((width, k), bf16),
            pltpu.VMEM((k, width), bf16),
            pltpu.VMEM((k, n), f32),
            pltpu.VMEM((k, n), bf16),
            pltpu.VMEM((groups, width, GROUP), f32),
            pltpu.VMEM((groups, width, GROUP), bf16),
            pltpu.VMEM((ROUNDS, chunks, 8, w), f32),
            pltpu.VMEM((ROUNDS, chunks, ncent - 1, 8, w), f32),
            pltpu.VMEM((8, n), f32),
            pltpu.VMEM((8, n), f32),
            pltpu.VMEM((ROUNDS - 1, groups, LANES), f32),
            pltpu.VMEM((ROUNDS - 1, ndp - 1, groups, LANES), f32),
            pltpu.VMEM((groups, LANES), f32),
            pltpu.VMEM((ndp - 1, groups, LANES), f32),
            pltpu.VMEM((chunks, k, LANES), f32),
            pltpu.VMEM((chunks, k, LANES), f32),
            pltpu.VMEM((k, LANES), f32),
            pltpu.VMEM((groups, ndp - 1, own, GROUP), bf16),
            dma,
            dma((E_PARTS,)),
            dma((2 * HALVES, line - 1)),
            dma((2 * HALVES,)),
            dma((2 * HALVES,)),
            dma((ROUNDS, chunks)),
            dma((ROUNDS, chunks)),
            dma((ROUNDS - 1,)),
            dma((ROUNDS - 1,)),
            dma,
            dma,
            dma((groups,)),
            dma((groups,)),
        ],
        compiler_params=pltpu.CompilerParams(
            collective_id=0, has_side_effects=True, vmem_limit_bytes=60 * 2**20
        ),
        name="sinkhorn",
    )(embeddings, centroids)
    return out.T


def solution(mesh):
    return jax.shard_map(
        body,
        mesh=mesh,
        in_specs=(P("dp", None), P("cent", "dp")),
        out_specs=P("cent", "dp"),
        check_vma=False,
    )
```

time: 76 us -> 63.6 us (0.84)
  Pallas kernels: 72.5 us -> 60.3 us
    pallas_call x1, Pallas kernels: 72.5 us -> 60.3 us  [body(): pl.pallas_call(functools.partial(kernel, ndp, ncent, chunks), out_shape=j...]
where the time goes in v2:
time: 63.6 us; the launch traced here: 63.4 us
  Pallas kernels  60.3 us (95%)
  local copies, waits for them, and re-layouts  3.08 us (5%)
    pallas_call x1, Pallas kernels, body(): pl.pallas_call(functools.partial(kernel, ndp, ncent, chunks), out_shape=j...  60.3 us
    unnamed x2, local copies, waits for them, and re-layouts  3.08 us

profile of v2, /device:TPU:0, one launch (start us, length us, event | category | flops | bytes accessed | tf_op | source)
XLA Modules:
  0.0 63.4 jit_solution(10545199459452614673)
XLA Ops:
  0.0 1.5 %copy.3.c_hbm = bf16[512,48]{1,0:T(8,128)(2,1)} copy(bf16[512,48]{0,1:T(8,128)(2,1)} %param.3) | data formatting | bytes 98304 | tf_op args[1]
  1.5 60.3 %sinkhorn.1 = f32[48,512]{1,0:T(8,128)} custom-call(bf16[4096,768]{1,0:T(8,128)(2,1)} %e_hbm.1, bf16[512,48]{1,0:T(8,128)(2,1)} %copy.3.c_hbm), custom_call_target="tpu_custom_call" | custom-call | tf_op jit(solution)/shard_map/sinkhorn/pallas_call | solution.py:360
  61.9 1.5 %copy.5 = f32[512,48]{0,1:T(8,128)} copy(f32[512,48]{0,1:T(8,128)} %bitcast.1) | data formatting | bytes 196608

commit v3 on v2

--- a/solution.py
+++ b/solution.py
@@ -42,7 +42,7 @@
 def kernel(
     ndp, ncent, chunks,
     e_hbm, c_hbm, out_ref,
-    c_in, e, ct_own, ct, c, b, plan, sums, low,
+    e, ct_own, ct, c, b, plan, sums, low,
     row_own, row_in, acc8, pot,
     col_own, col_in, mass_own, mass_in,
     peak, fac, part, rs_in,
@@ -79,7 +79,7 @@
     for o in range(1, ncent):
         pl.semaphore_signal(barrier, inc=1, device_id={"cent": cent_peer(o)}, device_id_type=MESH)
 
-    c_copy = pltpu.make_async_copy(c_hbm, c_in, c_sem)
+    c_copy = pltpu.make_async_copy(c_hbm, ct_own, c_sem)
     c_copy.start()
     e_copies = []
     step = n // E_PARTS
@@ -88,11 +88,7 @@
         e_copies.append(pltpu.make_async_copy(e_hbm.at[rows], e.at[rows], e_sem.at[i]))
         e_copies[-1].start()
 
-    eye = (
-        lax.broadcasted_iota(jnp.int32, (own, own), 0) == lax.broadcasted_iota(jnp.int32, (own, own), 1)
-    ).astype(f32).astype(bf16)
     c_copy.wait()
-    ct_own[...] = nt_dot(eye, c_in[...]).astype(bf16)
 
     def feats_of(dp):
         return pl.ds(pl.multiple_of(dp * own, own), own)
@@ -102,39 +98,44 @@
 
     pl.semaphore_wait(barrier, len(offsets) + ncent - 1)
 
-    quarters = 2 * HALVES
-    quart = k // quarters
-
-    def line(q, first):
-        if (q % 2 == 0) == first:
-            return [(d, 0) for d in range(1, nz)]
-        return [(0, d) for d in range(1, ny)]
-
-    def send_ct(q, src, rows, off, sem):
-        cols = pl.ds(q * quart, quart)
+    def hops(d, size):
+        return min(d, size - d)
+
+    def routes(dz, dy):
+        a, b_ = hops(dz, nz), hops(dy, ny)
+        if a == b_ and a > 1:
+            return (0, half // 2), (half // 2, half)
+        if a > b_ or (a == b_ and dz == dy):
+            return (0, half), None
+        return None, (0, half)
+
+    def send_ct(h, src, rows, part_, off, sem):
+        cols = pl.ds(h * half + part_[0], part_[1] - part_[0])
         pltpu.make_async_remote_copy(
-            src_ref=src.at[:, cols] if src is ct_own else src.at[rows, cols], dst_ref=ct.at[rows, cols],
-            send_sem=ct_send.at[q], recv_sem=sem,
+            src_ref=ct_own.at[:, cols] if src is ct_own else src.at[rows, cols], dst_ref=ct.at[rows, cols],
+            send_sem=ct_send.at[h], recv_sem=sem,
             device_id={"dp": dp_peer(*off)}, device_id_type=MESH,
         ).start()
 
-    def wait_ct(sem, q, blocks):
-        part_ = ct.at[pl.ds(0, own * blocks), pl.ds(q * quart, quart)]
+    def wait_ct(sem, h, blocks):
+        part_ = ct.at[pl.ds(0, own * blocks), pl.ds(h * half, half)]
         pltpu.make_async_copy(part_, part_, sem).wait()
 
-    for q in range(quarters):
-        for j, off in enumerate(line(q, True)):
-            send_ct(q, ct_own, mine, off, near_recv.at[q, j])
-        for off in line(q, False):
-            send_ct(q, ct_own, mine, off, ct_recv.at[q])
-        pending.append(functools.partial(wait_ct, ct_send.at[q], q, ndp - 1))
-    for q in range(quarters):
-        near = line(q, True)
-        order = sorted(range(len(near)), key=lambda j: min(j + 1, len(near) - j))
-        for j in order:
-            wait_ct(near_recv.at[q, len(near) - 1 - j], q, 1)
-            for off in line(q, False):
-                send_ct(q, ct, feats_of(dp_peer(*near[j])), off, ct_recv.at[q])
+    lines = [(d, 0) for d in range(1, nz)] + [(0, d) for d in range(1, ny)]
+    far_first = sorted(lines, key=lambda o: -hops(o[0], nz) - hops(o[1], ny))
+    for h in range(HALVES):
+        for off in far_first:
+            send_ct(h, ct_own, mine, (0, half), off, near_recv.at[h, lines.index(off)])
+        pending.append(functools.partial(wait_ct, ct_send.at[h], h, ndp - 1))
+    for h in range(HALVES):
+        for dz, dy in far_first[::-1]:
+            wait_ct(near_recv.at[h, lines.index((dz, dy))], h, 1)
+            rows = feats_of(dp_peer(nz - dz, ny - dy))
+            for d in range(1, ny if dy == 0 else nz):
+                off, both = ((0, d), (dz, d)) if dy == 0 else ((d, 0), (d, dy))
+                part_ = routes(*both)[0 if dy == 0 else 1]
+                if part_:
+                    send_ct(h, ct, rows, part_, off, ct_recv.at[h])
 
     unit = 4.0 / math.sqrt(width) / math.log(2.0)
     wide = 2 * w
@@ -152,17 +153,16 @@
         part_ = row_in.at[r, ch]
         pltpu.make_async_copy(part_, part_, sem.at[r, ch]).wait()
 
+    for copy in e_copies:
+        copy.wait()
     for h in range(HALVES):
-        for q in (2 * h, 2 * h + 1):
-            wait_ct(ct_recv.at[q], q, ndp - 1 - len(line(q, True)))
+        wait_ct(ct_recv.at[h], h, ndp - 1 - len(lines))
         rows = pl.ds(h * half, half)
         c[rows, :] = ct[:, rows].T
         for ch in range(chunks):
             for i in range(0, 8, 2):
                 at = (ch * 8 + i) * w
                 toks = pl.ds(at, wide)
-                if h == 0 and at % step == 0:
-                    e_copies[at // step].wait()
                 x = nt_dot(c[rows, :], e[toks, :]) * unit
                 b[rows, toks] = x
                 top = jnp.max(x, axis=0, keepdims=True)
@@ -349,9 +349,12 @@
 
 
 def body(embeddings, centroids):
+    centroids = centroids.T
+    embeddings = pltpu.with_memory_space_constraint(embeddings, pltpu.HBM)
+    centroids = pltpu.with_memory_space_constraint(centroids, pltpu.HBM)
     ndp, ncent = lax.axis_size("dp"), lax.axis_size("cent")
     n, width = embeddings.shape
-    k, own = centroids.shape
+    own, k = centroids.shape
     chunks = 2
     w = n // (8 * chunks)
     groups = k // GROUP
@@ -359,11 +362,10 @@
     dma = pltpu.SemaphoreType.DMA
     out = pl.pallas_call(
         functools.partial(kernel, ndp, ncent, chunks),
-        out_shape=jax.ShapeDtypeStruct((own, k), f32),
+        out_shape=pltpu.VMEM((own, k), f32),
         in_specs=[pl.BlockSpec(memory_space=pl.ANY), pl.BlockSpec(memory_space=pl.ANY)],
         out_specs=pl.BlockSpec(memory_space=pltpu.VMEM),
         scratch_shapes=[
-            pltpu.VMEM((k, own), bf16),
             pltpu.VMEM((n, width), bf16),
             pltpu.VMEM((own, k), bf16),
             pltpu.VMEM((width, k), bf16),
@@ -386,9 +388,9 @@
             pltpu.VMEM((groups, ndp - 1, own, GROUP), bf16),
             dma,
             dma((E_PARTS,)),
-            dma((2 * HALVES, line - 1)),
-            dma((2 * HALVES,)),
-            dma((2 * HALVES,)),
+            dma((HALVES, 2 * (line - 1))),
+            dma((HALVES,)),
+            dma((HALVES,)),
             dma((ROUNDS, chunks)),
             dma((ROUNDS, chunks)),
             dma((ROUNDS - 1,)),
@@ -399,7 +401,7 @@
             dma((groups,)),
         ],
         compiler_params=pltpu.CompilerParams(
-            collective_id=0, has_side_effects=True, vmem_limit_bytes=60 * 2**20
+            collective_id=0, has_side_effects=True, vmem_limit_bytes=50 * 2**20
         ),
         name="sinkhorn",
     )(embeddings, centroids)

time: 63.6 us -> 59.1 us (0.929)
  local copies, waits for them, and re-layouts: 3.08 us -> 0.64 us
  Pallas kernels: 60.3 us -> 58.4 us
    unnamed x2 -> x1, local copies, waits for them, and re-layouts: 3.08 us -> 0.64 us
    pallas_call x1, Pallas kernels: 60.3 us -> 58.4 us  [body(): pl.pallas_call(functools.partial(kernel, ndp, ncent, chunks), out_shape=p...]
where the time goes in v3:
time: 59.1 us; the launch traced here: 59 us
  Pallas kernels  58.4 us (99%)
  local copies, waits for them, and re-layouts  0.64 us (1%)
    pallas_call x1, Pallas kernels, body(): pl.pallas_call(functools.partial(kernel, ndp, ncent, chunks), out_shape=p...  58.4 us

profile of v3, /device:TPU:0, one launch (start us, length us, event | category | flops | bytes accessed | tf_op | source)
XLA Modules:
  0.0 59.0 jit_solution(11350614373137547028)
XLA Ops:
  0.0 58.4 %sinkhorn.1 = f32[48,512]{1,0:T(8,128)S(1)} custom-call(bf16[4096,768]{1,0:T(8,128)(2,1)} %e_hbm.1, bf16[48,512]{1,0:T(8,128)(2,1)} %bitcast.3), custom_call_target="tpu_custom_call" | custom-call | tf_op jit(solution)/shard_map/sinkhorn/pallas_call | solution.py:363
  58.4 0.6 %copy.4 = f32[512,48]{0,1:T(8,128)} copy(f32[512,48]{0,1:T(8,128)S(1)} %bitcast.2) | data formatting | bytes 196608

commit v4 on v3

--- a/solution.py
+++ b/solution.py
@@ -31,8 +31,8 @@
     return top + jnp.log2(functools.reduce(jnp.add, [jnp.exp2(p - top) for p in parts]))
 
 
-def to_lanes(col):
-    return jnp.broadcast_to(col, (GROUP, LANES)).T[0:1, :]
+def lane_sums(a):
+    return jnp.sum(a.T, axis=0, keepdims=True)
 
 
 def to_rows(row):
@@ -45,9 +45,9 @@
     e, ct_own, ct, c, b, plan, sums, low,
     row_own, row_in, acc8, pot,
     col_own, col_in, mass_own, mass_in,
-    peak, fac, part, rs_in,
+    peak, fac, part, diag_in, line_out, line_in,
     c_sem, e_sem, near_recv, ct_send, ct_recv, row_send, row_recv, col_send, col_recv,
-    mass_send, mass_recv, rs_send, rs_recv,
+    mass_send, mass_recv, diag_send, diag_recv, line_send, line_recv,
 ):
     n, width = e.shape
     k = c.shape[0]
@@ -65,22 +65,29 @@
     mec = lax.axis_index("cent")
     my_z, my_y = me // ny, me % ny
 
+    def hops(d, size):
+        return min(d, size - d)
+
     offsets = [(dz, dy) for dz in range(nz) for dy in range(ny)][1:]
+    offsets.sort(key=lambda o: -hops(o[0], nz) - hops(o[1], ny))
+    nx = ncent // 2
+    cent_offsets = [(dx, core) for dx in range(nx) for core in range(2)][1:]
+    cent_offsets.sort(key=lambda o: -hops(o[0], nx))
 
     def dp_peer(dz, dy):
         return ((my_z + dz) % nz) * ny + (my_y + dy) % ny
 
-    def cent_peer(o):
-        return (mec + o) % ncent
-
+    def cent_peer(dx, core):
+        return ((mec // 2 + dx) % nx) * 2 + (mec + core) % 2
+
+    c_copy = pltpu.make_async_copy(c_hbm, ct_own, c_sem)
+    c_copy.start()
     barrier = pltpu.get_barrier_semaphore()
     for dz, dy in offsets:
         pl.semaphore_signal(barrier, inc=1, device_id={"dp": dp_peer(dz, dy)}, device_id_type=MESH)
-    for o in range(1, ncent):
-        pl.semaphore_signal(barrier, inc=1, device_id={"cent": cent_peer(o)}, device_id_type=MESH)
-
-    c_copy = pltpu.make_async_copy(c_hbm, ct_own, c_sem)
-    c_copy.start()
+    for o in cent_offsets:
+        pl.semaphore_signal(barrier, inc=1, device_id={"cent": cent_peer(*o)}, device_id_type=MESH)
+
     e_copies = []
     step = n // E_PARTS
     for i in range(E_PARTS):
@@ -97,9 +104,6 @@
     ct[mine, :] = ct_own[...]
 
     pl.semaphore_wait(barrier, len(offsets) + ncent - 1)
-
-    def hops(d, size):
-        return min(d, size - d)
 
     def routes(dz, dy):
         a, b_ = hops(dz, nz), hops(dy, ny)
@@ -141,11 +145,11 @@
     wide = 2 * w
 
     def send_rows(r, ch):
-        for o in range(1, ncent):
+        for j, o in enumerate(cent_offsets):
             pltpu.make_async_remote_copy(
-                src_ref=row_own.at[r, ch], dst_ref=row_in.at[r, ch, o - 1],
+                src_ref=row_own.at[r, ch], dst_ref=row_in.at[r, ch, j],
                 send_sem=row_send.at[r, ch], recv_sem=row_recv.at[r, ch],
-                device_id={"cent": cent_peer(o)}, device_id_type=MESH,
+                device_id={"cent": cent_peer(*o)}, device_id_type=MESH,
             ).start()
         pending.append(lambda: wait_rows(row_send, r, ch))
 
@@ -221,7 +225,7 @@
                 return a + x
 
             a = over_tiles(exp_step, jnp.zeros((GROUP, LANES), f32))
-            lse = to_lanes(m[:, 0:1] + jnp.log2(jnp.sum(a, axis=1, keepdims=True)))
+            lse = m.T[0:1, :] + jnp.log2(lane_sums(a))
             if ch > 0:
                 lse = lse2([lse, col_own[0, g : g + 1, :]])
             col_own[0, g : g + 1, :] = lse
@@ -275,7 +279,7 @@
             if ch < chunks - 1:
                 part[gs, :] = a
             else:
-                col_own[1, g : g + 1, :] = to_lanes(jnp.sum(a, axis=1, keepdims=True))
+                col_own[1, g : g + 1, :] = lane_sums(a)
     send_cols(1)
     wait_cols(col_recv, 1)
     tot = col_own[1]
@@ -288,64 +292,95 @@
         for ch in range(chunks):
             fac[ch, gs, :] = fac[ch, gs, :] * scale
 
+    def make_plan(ch, g):
+        gs = pl.ds(g * GROUP, GROUP)
+        f = fac[ch, gs, :]
+
+        def plan_step(i, a):
+            x = (b[gs, tile(ch, i)] * f) * pot[0:1, tile(ch, i)]
+            plan[gs, tile(ch, i)] = x.astype(bf16)
+            return a + x
+
+        a = over_tiles(plan_step, jnp.zeros((GROUP, LANES), f32))
+        if ch > 0:
+            a = a + part[gs, :]
+        if ch < chunks - 1:
+            part[gs, :] = a
+        else:
+            mass_own[g : g + 1, :] = lane_sums(a)
+
     send_row_sums(2)
     for ch in range(chunks):
         take_row_sums(2, ch)
-
-    def make_plan(g):
-        gs = pl.ds(g * GROUP, GROUP)
-        a = jnp.zeros((GROUP, LANES), f32)
-        for ch in range(chunks):
-            f = fac[ch, gs, :]
-
-            def plan_step(i, a):
-                x = (b[gs, tile(ch, i)] * f) * pot[0:1, tile(ch, i)]
-                plan[gs, tile(ch, i)] = x.astype(bf16)
-                return a + x
-
-            a = over_tiles(plan_step, a)
-        mass_own[g : g + 1, :] = to_lanes(jnp.sum(a, axis=1, keepdims=True))
-
-    def wait_sums(sem, g):
-        part_ = rs_in.at[g]
-        pltpu.make_async_copy(part_, part_, sem.at[g]).wait()
-
-    make_plan(0)
+        for g in range(groups if ch < chunks - 1 else 1):
+            make_plan(ch, g)
+
+    def wait_all(buf, sem):
+        pltpu.make_async_copy(buf, buf, sem).wait()
+
+    diag = [o for o in offsets if o[0] and o[1]]
+
+    def by_z(g, dz, dy):
+        a, b_ = hops(dz, nz), hops(dy, ny)
+        if a == b_:
+            return dz == dy if a == 1 else g % 2 == 0
+        return a < b_
+
+    def send_sums(src, dst, sems, g, peer):
+        pltpu.make_async_remote_copy(
+            src_ref=src, dst_ref=dst, send_sem=sems[0].at[g], recv_sem=sems[1].at[g],
+            device_id={"dp": peer}, device_id_type=MESH,
+        ).start()
+
+    def start_sums(g):
+        for j, (dz, dy) in enumerate(diag):
+            there = dp_peer(dz, 0) if by_z(g, dz, dy) else dp_peer(0, dy)
+            send_sums(low.at[g, feats_of(dp_peer(dz, dy)), :], diag_in.at[g, j], (diag_send, diag_recv), g, there)
+        pending.append(functools.partial(wait_all, diag_in.at[g], diag_send.at[g]))
+
+    def pass_sums(g):
+        wait_all(diag_in.at[g], diag_recv.at[g])
+        for j, off in enumerate(far_first):
+            peer = dp_peer(*off)
+            tot = sums[g, feats_of(peer), :]
+            for i, (dz, dy) in enumerate(diag):
+                if off == ((0, dy) if by_z(g, dz, dy) else (dz, 0)):
+                    tot = tot + diag_in[g, i].astype(f32)
+            line_out[g, j] = tot
+            send_sums(line_out.at[g, j], line_in.at[g, j], (line_send, line_recv), g, peer)
+
     for g in range(groups):
         if g + 1 < groups:
-            make_plan(g + 1)
+            make_plan(chunks - 1, g + 1)
         s = nn_dot(plan[pl.ds(g * GROUP, GROUP), :], e[...]).T
         sums[g] = s
         low[g] = s.astype(bf16)
-        for o, (dz, dy) in enumerate(offsets):
-            peer = dp_peer(dz, dy)
-            pltpu.make_async_remote_copy(
-                src_ref=low.at[g, feats_of(peer), :], dst_ref=rs_in.at[g, o],
-                send_sem=rs_send.at[g], recv_sem=rs_recv.at[g],
-                device_id={"dp": peer}, device_id_type=MESH,
-            ).start()
-        pending.append(functools.partial(wait_sums, rs_send, g))
+        start_sums(g)
         if g == max(groups - 2, 0):
             for o, (dz, dy) in enumerate(offsets):
                 pltpu.make_async_remote_copy(
                     src_ref=mass_own, dst_ref=mass_in.at[o], send_sem=mass_send, recv_sem=mass_recv,
                     device_id={"dp": dp_peer(dz, dy)}, device_id_type=MESH,
                 ).start()
-            pending.append(lambda: pltpu.make_async_copy(mass_in, mass_in, mass_send).wait())
-
-    pltpu.make_async_copy(mass_in, mass_in, mass_recv).wait()
+            pending.append(lambda: wait_all(mass_in, mass_send))
+    for g in range(groups):
+        pass_sums(g)
+
+    for wait in pending:
+        wait()
+
+    wait_all(mass_in, mass_recv)
     mass = mass_own[...]
     for j in range(ndp - 1):
         mass = mass + mass_in[j]
     for g in range(groups):
-        wait_sums(rs_recv, g)
         tot = sums[g, mine, :]
-        for j in range(ndp - 1):
-            tot = tot + rs_in[g, j].astype(f32)
+        wait_all(line_in.at[g], line_recv.at[g])
+        for j in range(len(lines)):
+            tot = tot + line_in[g, j]
         out_ref[:, pl.ds(g * GROUP, GROUP)] = tot / mass[g : g + 1, :]
-
-    for wait in pending:
-        wait()
+    for g in range(groups):
+        wait_all(line_in.at[g], line_send.at[g])
 
 
 def body(embeddings, centroids):
@@ -385,7 +420,9 @@
             pltpu.VMEM((chunks, k, LANES), f32),
             pltpu.VMEM((chunks, k, LANES), f32),
             pltpu.VMEM((k, LANES), f32),
-            pltpu.VMEM((groups, ndp - 1, own, GROUP), bf16),
+            pltpu.VMEM((groups, (line - 1) ** 2, own, GROUP), bf16),
+            pltpu.VMEM((groups, 2 * (line - 1), own, GROUP), f32),
+            pltpu.VMEM((groups, 2 * (line - 1), own, GROUP), f32),
             dma,
             dma((E_PARTS,)),
             dma((HALVES, 2 * (line - 1))),
@@ -399,6 +436,8 @@
             dma,
             dma((groups,)),
             dma((groups,)),
+            dma((groups,)),
+            dma((groups,)),
         ],
         compiler_params=pltpu.CompilerParams(
             collective_id=0, has_side_effects=True, vmem_limit_bytes=50 * 2**20

time: 59.1 us -> 58.2 us (0.985)
  Pallas kernels: 58.4 us -> 57.5 us
    pallas_call x1, Pallas kernels: 58.4 us -> 57.5 us  [body(): pl.pallas_call(functools.partial(kernel, ndp, ncent, chunks), out_shape=p...]
where the time goes in v4:
time: 58.2 us; the launch traced here: 58.1 us
  Pallas kernels  57.5 us (99%)
  local copies, waits for them, and re-layouts  0.64 us (1%)
    pallas_call x1, Pallas kernels, body(): pl.pallas_call(functools.partial(kernel, ndp, ncent, chunks), out_shape=p...  57.5 us

profile of v4, /device:TPU:0, one launch (start us, length us, event | category | flops | bytes accessed | tf_op | source)
XLA Modules:
  0.0 58.1 jit_solution(17497653758188227754)
XLA Ops:
  0.0 57.5 %sinkhorn.1 = f32[48,512]{1,0:T(8,128)S(1)} custom-call(bf16[4096,768]{1,0:T(8,128)(2,1)} %e_hbm.1, bf16[48,512]{1,0:T(8,128)(2,1)} %bitcast.3), custom_call_target="tpu_custom_call" | custom-call | tf_op jit(solution)/shard_map/sinkhorn/pallas_call | solution.py:398
  57.5 0.6 %copy.4 = f32[512,48]{0,1:T(8,128)} copy(f32[512,48]{0,1:T(8,128)S(1)} %bitcast.2) | data formatting | bytes 196608

commit v5 on v4

--- a/solution.py
+++ b/solution.py
@@ -159,11 +159,12 @@
 
     for copy in e_copies:
         copy.wait()
-    for h in range(HALVES):
-        wait_ct(ct_recv.at[h], h, ndp - 1 - len(lines))
-        rows = pl.ds(h * half, half)
-        c[rows, :] = ct[:, rows].T
-        for ch in range(chunks):
+    for ch in range(chunks):
+        for h in range(HALVES):
+            rows = pl.ds(h * half, half)
+            if ch == 0:
+                wait_ct(ct_recv.at[h], h, ndp - 1 - len(lines))
+                c[rows, :] = ct[:, rows].T
             for i in range(0, 8, 2):
                 at = (ch * 8 + i) * w
                 toks = pl.ds(at, wide)
@@ -178,8 +179,7 @@
                     lse = lse2([lse, acc8[0:1, toks]])
                     row_own[0, ch, i : i + 1, :] = lse[:, :w]
                     row_own[0, ch, i + 1 : i + 2, :] = lse[:, w:]
-            if h == HALVES - 1:
-                send_rows(0, ch)
+        send_rows(0, ch)
 
     tiles = n // (chunks * LANES)
 

time: 58.2 us -> 58.1 us (level)
  no operation moved by 1% of the time
where the time goes in v5:
time: 58.1 us; the launch traced here: 58 us
  Pallas kernels  57.4 us (99%)
  local copies, waits for them, and re-layouts  0.64 us (1%)
    pallas_call x1, Pallas kernels, body(): pl.pallas_call(functools.partial(kernel, ndp, ncent, chunks), out_shape=p...  57.4 us

profile of v5, /device:TPU:0, one launch (start us, length us, event | category | flops | bytes accessed | tf_op | source)
XLA Modules:
  0.0 58.0 jit_solution(3171072033725020889)
XLA Ops:
  0.0 57.4 %sinkhorn.1 = f32[48,512]{1,0:T(8,128)S(1)} custom-call(bf16[4096,768]{1,0:T(8,128)(2,1)} %e_hbm.1, bf16[48,512]{1,0:T(8,128)(2,1)} %bitcast.3), custom_call_target="tpu_custom_call" | custom-call | tf_op jit(solution)/shard_map/sinkhorn/pallas_call | solution.py:398
  57.4 0.6 %copy.4 = f32[512,48]{0,1:T(8,128)} copy(f32[512,48]{0,1:T(8,128)S(1)} %bitcast.2) | data formatting | bytes 196608

commit v6 on v5

--- a/solution.py
+++ b/solution.py
@@ -356,13 +356,12 @@
         sums[g] = s
         low[g] = s.astype(bf16)
         start_sums(g)
-        if g == max(groups - 2, 0):
-            for o, (dz, dy) in enumerate(offsets):
-                pltpu.make_async_remote_copy(
-                    src_ref=mass_own, dst_ref=mass_in.at[o], send_sem=mass_send, recv_sem=mass_recv,
-                    device_id={"dp": dp_peer(dz, dy)}, device_id_type=MESH,
-                ).start()
-            pending.append(lambda: wait_all(mass_in, mass_send))
+    for o, (dz, dy) in enumerate(offsets):
+        pltpu.make_async_remote_copy(
+            src_ref=mass_own, dst_ref=mass_in.at[o], send_sem=mass_send, recv_sem=mass_recv,
+            device_id={"dp": dp_peer(dz, dy)}, device_id_type=MESH,
+        ).start()
+    pending.append(lambda: wait_all(mass_in, mass_send))
     for g in range(groups):
         pass_sums(g)
 

time: 58.1 us -> 58.4 us (level)
  no operation moved by 1% of the time
where the time goes in v6:
time: 58.4 us; the launch traced here: 58 us
  Pallas kernels  57.3 us (98%)
  local copies, waits for them, and re-layouts  0.64 us (1%)
    pallas_call x1, Pallas kernels, body(): pl.pallas_call(functools.partial(kernel, ndp, ncent, chunks), out_shape=p...  57.3 us

profile of v6, /device:TPU:0, one launch (start us, length us, event | category | flops | bytes accessed | tf_op | source)
XLA Modules:
  0.0 58.0 jit_solution(8394647147382703287)
XLA Ops:
  0.0 57.3 %sinkhorn.1 = f32[48,512]{1,0:T(8,128)S(1)} custom-call(bf16[4096,768]{1,0:T(8,128)(2,1)} %e_hbm.1, bf16[48,512]{1,0:T(8,128)(2,1)} %bitcast.3), custom_call_target="tpu_custom_call" | custom-call | tf_op jit(solution)/shard_map/sinkhorn/pallas_call | solution.py:397
  57.3 0.6 %copy.4 = f32[512,48]{0,1:T(8,128)} copy(f32[512,48]{0,1:T(8,128)S(1)} %bitcast.2) | data formatting | bytes 196608
